TPU v7x, 128 devices: a whole 4x4x4 slice. The times are simulated.
128 devices in a mesh: user: 8 (over x, z_hi), item: 16 (over z_lo, y, core).
Axes of the slice: x: 4, y: 4, z: 4 (z_hi: 2, z_lo: 2; z = z_hi * 2 + z_lo), core: 2. Of those that a mesh axis runs over, the one named last changes fastest.
Arguments:
- counts: int32 [16384, 24576], P('user', 'item'), may hold values from 0 to 3
- user_factors: bfloat16 [16384, 256], P('user', 'item'), may hold values from -1.1953125 to 1.1953125
- item_factors: bfloat16 [24576, 256], P('item', 'user'), may hold values from -1.1953125 to 1.1953125
- alpha_scale: float32 [1], replicated, may hold values from 0.5 to 2
Outputs:
- user_new: float32 [16384, 256], P('user', 'item')
- item_new: float32 [24576, 256], P('item', 'user')
All inputs are finite; a program needn't handle non-finite values.
Results may differ from a plain program's by a relative error of at most 0.0021.
Values may be sent and summed in bfloat16 or wider, within the bound.
A program may use at most 128 MiB of HBM per device.

v0:
```python
import jax
import jax.numpy as jnp
from jax import lax
from jax.sharding import PartitionSpec as P

reg_weight = 1.0


def newton(gram_matrix, gradient):
    bound = 0.25 * gram_matrix + reg_weight * jnp.eye(gram_matrix.shape[0], dtype=jnp.float32)
    factor_low = jnp.linalg.cholesky(bound)
    return jax.scipy.linalg.cho_solve((factor_low, True), gradient.T).T


def coefficients(count_block, scale, left, right):
    scores = jnp.einsum("ud,id->ui", left, right, preferred_element_type=jnp.float32)
    weight = scale * count_block.astype(jnp.float32)
    return (weight - (1.0 + weight) * jax.nn.sigmoid(scores)).astype(jnp.bfloat16)


def gram_of(factor_rows):
    return jnp.einsum("nd,ne->de", factor_rows, factor_rows, preferred_element_type=jnp.float32)


def on_device(counts, user_factors, item_factors, alpha_scale):
    scale = alpha_scale[0]
    user_ways = lax.axis_size("user")
    item_ways = lax.axis_size("item")
    user_full = lax.all_gather(user_factors, "item", axis=1, tiled=True)
    item_full = lax.all_gather(item_factors, "user", axis=1, tiled=True)
    coefficient = coefficients(counts, scale, user_full, item_full)
    gram_items = lax.psum(gram_of(item_full), "item")
    gradient = lax.psum(jnp.dot(coefficient, item_full, preferred_element_type=jnp.float32), "item")
    gradient = gradient - reg_weight * user_full.astype(jnp.float32)
    user_new = user_full.astype(jnp.float32) + newton(gram_items, gradient)
    user_half = user_new.astype(jnp.bfloat16)
    user_width = user_new.shape[1] // item_ways
    user_out = lax.dynamic_slice_in_dim(
        user_new, lax.axis_index("item") * user_width, user_width, 1
    )
    coefficient_next = coefficients(counts, scale, user_half, item_full)
    gram_users = lax.psum(gram_of(user_half), "user")
    item_grad = lax.psum(
        jnp.einsum("ui,ud->id", coefficient_next, user_half, preferred_element_type=jnp.float32),
        "user",
    )
    item_grad = item_grad - reg_weight * item_full.astype(jnp.float32)
    item_new = item_full.astype(jnp.float32) + newton(gram_users, item_grad)
    item_width = item_new.shape[1] // user_ways
    item_out = lax.dynamic_slice_in_dim(
        item_new, lax.axis_index("user") * item_width, item_width, 1
    )
    return (user_out, item_out)


def solution(mesh):
    in_specs = (P("user", "item"), P("user", "item"), P("item", "user"), P())
    out_specs = (P("user", "item"), P("item", "user"))
    return jax.shard_map(
        on_device, mesh=mesh, in_specs=in_specs, out_specs=out_specs, check_vma=False
    )
```

profile of v0, /device:TPU:0, one launch (start us, length us, event | category | flops | bytes accessed | tf_op | source)
XLA Modules:
  0.0 453.1 jit_solution(4885983498665630628)
XLA Ops:
  8.6 36.5 %all_gather.7 = bf16[1536,256]{0,1:T(8,128)(2,1)S(1)} all-gather(bf16[1536,32]{0,1:T(8,128)(2,1)} %param.7), channel_id=1, replica_groups=mesh['user'=8,'item'=16] {'user'}, dimensions={1}, use_global_device_ids=true | all-gather | bytes 884736 | tf_op jit(solution)/shard_map/all_gather | solution.py:30
  45.1 1.1 fusion.33
  46.5 11.0 %fusion.1 = f32[2048,256]{1,0:T(8,128)} fusion(bf16[1536,256]{0,1:T(8,128)(2,1)S(1)} %all_gather.7, s32[2048,1536]{1,0:T(8,128)} %param.5, bf16[2048,256]{0,1:T(8,128)(2,1)} %all-gather.2.cloned.1.call-done, f32[]{:T(128)} %bitcast.90), kind=kOutput, calls=%fused_computation.14 | convolution fusion | flops 3249537024 | bytes 16515076 | tf_op jit(solution)/shard_map/dot_general | solution.py:33
  59.2 124.3 %all-reduce.6.cloned.1.call-done = (f32[2048,256]{1,0:T(8,128)}, f32[256,256]{0,1:T(8,128)}) async-done(((f32[2048,256]{1,0:T(8,128)}, f32[256,256]{0,1:T(8,128)}), (f32[2048,256]{1,0:T(8,128)}, f32[256,256]{0,1:T(8,128)})) %all-reduce.6.cloned.1.call-update) | async-done | bytes 2359312 | tf_op jit(solution)/shard_map/psum | solution.py:33
  185.7 11.7 %cholesky.130 = f32[128,128]{1,0:T(8,128)S(1)} custom-call(f32[128,128]{1,0:T(8,128)S(1)} %cholesky.194), custom_call_target="Cholesky" | custom-call | tf_op jit(solution)/shard_map/jit(cholesky)/cholesky | solution.py:11
  197.5 9.8 %custom-call.25 = f32[1,128,128]{1,2,0:T(8,128)S(1)} custom-call(f32[1,128,128]{2,1,0:T(8,128)S(1)} %get-tuple-element.54), custom_call_target="InvertDiagBlocksLowerTriangular" | custom-call | tf_op jit(solution)/shard_map/jit(cholesky)/cholesky | solution.py:11
  207.8 11.7 %cholesky.147 = f32[128,128]{1,0:T(8,128)S(1)} custom-call(f32[128,128]{1,0:T(8,128)S(1)} %convolution_subtract_fusion.5), custom_call_target="Cholesky" | custom-call | tf_op jit(solution)/shard_map/jit(cholesky)/cholesky | solution.py:11
  221.6 4.1 while.2
  222.3 1.3 bitcast_dynamic-update-slice_fusion.4
  224.3 1.3 bitcast_dynamic-update-slice_fusion.4
  225.7 20.1 %custom-call.22 = f32[2,128,128]{1,2,0:T(8,128)S(1)} custom-call(f32[2,128,128]{2,1,0:T(8,128)S(1)} %get-tuple-element.10), custom_call_target="InvertDiagBlocksLowerTriangular" | custom-call | tf_op jit(solution)/shard_map/jit(_cho_solve)/triangular_solve | solution.py:12
  245.8 1.8 fusion.2
  248.7 1.8 convolution_subtract_fusion.3
  252.6 1.3 copy.22
  255.0 1.8 fusion.19
  257.0 1.2 fusion.9
  258.3 12.1 %fusion = f32[1536,256]{1,0:T(8,128)} fusion(s32[2048,1536]{1,0:T(8,128)} %param.5, bf16[1536,256]{0,1:T(8,128)(2,1)S(1)} %all_gather.7, f32[]{:T(128)} %bitcast.89, f32[2048,256]{1,0:T(8,128)S(1)} %convert_add_fusion), kind=kOutput, calls=%fused_computation.13 | convolution fusion | flops 3250585600 | bytes 17039364 | tf_op jit(solution)/shard_map/ui,ud->id/dot_general | solution.py:44
  270.4 1.2 copy.23
  271.5 2.4 convert_element_type.31
  274.0 1.4 constant_dynamic-slice_fusion.2
  275.3 2.2 copy.28
  277.5 98.6 %all-reduce.8.cloned.1.call-done = (f32[1536,256]{1,0:T(8,128)}, f32[256,256]{0,1:T(8,128)}) async-done(((f32[1536,256]{1,0:T(8,128)}, f32[256,256]{0,1:T(8,128)}), (f32[1536,256]{1,0:T(8,128)}, f32[256,256]{0,1:T(8,128)})) %all-reduce.8.cloned.1.call-update) | async-done | bytes 1835024 | tf_op jit(solution)/shard_map/psum | solution.py:43
  376.1 1.6 subtract_bitcast_fusion
  377.9 11.7 %cholesky.164 = f32[128,128]{1,0:T(8,128)S(1)} custom-call(f32[128,128]{1,0:T(8,128)S(1)} %cholesky.197), custom_call_target="Cholesky" | custom-call | tf_op jit(solution)/shard_map/jit(cholesky)/cholesky | solution.py:11
  389.7 9.8 %custom-call.26 = f32[1,128,128]{1,2,0:T(8,128)S(1)} custom-call(f32[1,128,128]{2,1,0:T(8,128)S(1)} %get-tuple-element.50), custom_call_target="InvertDiagBlocksLowerTriangular" | custom-call | tf_op jit(solution)/shard_map/jit(cholesky)/cholesky | solution.py:11
  400.0 11.9 %cholesky.181 = f32[128,128]{1,0:T(8,128)S(1)} custom-call(f32[128,128]{1,0:T(8,128)S(1)} %convolution_subtract_fusion.4), custom_call_target="Cholesky" | custom-call | tf_op jit(solution)/shard_map/jit(cholesky)/cholesky | solution.py:11
  414.7 4.0 while.3
  415.3 1.4 bitcast_dynamic-update-slice_fusion.5
  417.3 1.4 bitcast_dynamic-update-slice_fusion.5
  418.7 19.7 %custom-call.23 = f32[2,128,128]{1,2,0:T(8,128)S(1)} custom-call(f32[2,128,128]{2,1,0:T(8,128)S(1)} %get-tuple-element.18), custom_call_target="InvertDiagBlocksLowerTriangular" | custom-call | tf_op jit(solution)/shard_map/jit(_cho_solve)/triangular_solve | solution.py:12
  439.2 1.4 convolution_subtract_fusion.1
  443.4 1.4 fusion.22
  (70 shorter events, 20.5 us)
Async XLA Ops:
  7.2 39.3 %all-gather.2.cloned.1.call-start = ((), (), s32[]{:S(2)}) async-start(), calls=%async_computation | async-start | bytes 1114112 | tf_op jit(solution)/shard_map/all_gather | solution.py:29
  7.9 175.7 %all-reduce.6.cloned.1.call-start = ((), (), s32[]{:S(2)}) async-start(), calls=%async_computation.1 | async-start | bytes 4718592 | tf_op jit(solution)/shard_map/psum | solution.py:33
  57.5 1.2 copy-start.6
  57.5 318.6 %all-reduce.8.cloned.1.call-start = ((), (), s32[]{:S(2)}) async-start(), calls=%async_computation.2 | async-start | bytes 3670016 | tf_op jit(solution)/shard_map/psum | solution.py:43
  59.2 186.6 %copy-start = (bf16[2048,256]{1,0:T(8,128)(2,1)}, bf16[2048,256]{1,0:T(8,128)(2,1)S(1)}, u32[]{:S(2)}) copy-start(bf16[2048,256]{1,0:T(8,128)(2,1)S(1)} %copy.18) | copy-start | bytes 3145732
  253.9 2.9 copy-start.1
  253.9 2.9 copy-start.3
  274.0 102.1 %copy-start.2 = (bf16[1536,256]{1,0:T(8,128)(2,1)S(1)}, bf16[1536,256]{1,0:T(8,128)(2,1)}, u32[]{:S(2)}) copy-start(bf16[1536,256]{1,0:T(8,128)(2,1)} %copy.23) | copy-start | bytes 2359300
  376.1 1.6 copy-start.5
  443.4 1.5 copy-start.4
Sparse Core Ops, SparseCore 0:
  9.7 36.7 all-gather.1
  57.6 125.8 all-reduce.5
  270.5 105.5 all-reduce.7
where the time goes:
time: 458 us; the launch traced here: 453 us
  waiting for transfers between devices  224 us (49%)
  other arithmetic  117 us (26%)
  matrix products  40.4 us (9%)
  blocking collectives  36.5 us (8%)
  between operations  17.5 us (4%)
  local copies, waits for them, and re-layouts  17.1 us (4%)
    psum x1, waiting for transfers between devices, on_device(): lax.psum(jnp.dot(coefficient, item_full, preferred_element_type=jnp.float...  124 us
    psum x1, waiting for transfers between devices, on_device(): lax.psum(jnp.einsum('ui,ud->id', coefficient_next, user_half, preferred_e...  98.6 us
    another operation x13, other arithmetic, newton(): factor_low = jnp.linalg.cholesky(bound)  68.9 us
    another operation x5, other arithmetic, newton(): return jax.scipy.linalg.cho_solve((factor_low, True), gradient.T).T  39.8 us
    all_gather x1, blocking collectives, on_device(): item_full = lax.all_gather(item_factors, 'user', axis=1, tiled=True)  36.5 us
    another operation x12, matrix products, newton(): return jax.scipy.linalg.cho_solve((factor_low, True), gradient.T).T  14 us
    dot_general x1, matrix products, on_device(): jnp.einsum('ui,ud->id', coefficient_next, user_half, preferred_element_ty...  12.1 us
    dot_general x1, matrix products, on_device(): jnp.dot(coefficient, item_full, preferred_element_type=jnp.float32)  11 us
  transfers between devices with their start and end apart: 3, of which 3 were waited for; matrix products, arithmetic and copies ran while one was open for 2% of the time, Pallas kernels for 0%

commit v1 on v0

v1 whole, which is shorter than its diff:
```python
import functools

import jax
import jax.numpy as jnp
from jax import lax
from jax.experimental import pallas as pl
from jax.experimental.pallas import tpu as pltpu
from jax.sharding import PartitionSpec as P

MESH = pl.DeviceIdType.MESH
EXACT = lax.Precision.HIGHEST
F32 = jnp.float32
BF16 = jnp.bfloat16
TN = (((0,), (0,)), ((), ()))
REG = 1.0
PANEL = 32
LANES = 128
TILE = 16


def eye(n):
    return lax.broadcasted_iota(jnp.int32, (n, n), 0) == lax.broadcasted_iota(
        jnp.int32, (n, n), 1
    )


def invert(a_ref):
    n = a_ref.shape[0]
    ri = lax.broadcasted_iota(jnp.int32, (n, n), 0)
    ci = lax.broadcasted_iota(jnp.int32, (n, n), 1)
    h = a_ref[...]
    diagonal = jnp.where(ri == ci, h, 0.0)
    s_row = lax.rsqrt(jnp.sum(diagonal, axis=0, keepdims=True))
    s_col = lax.rsqrt(jnp.sum(diagonal, axis=1, keepdims=True))
    a_ref[...] = h * s_row * s_col
    lr = lax.broadcasted_iota(jnp.int32, (PANEL, n), 0)
    lc = lax.broadcasted_iota(jnp.int32, (PANEL, n), 1)
    sub = lax.broadcasted_iota(jnp.int32, (PANEL, LANES), 0)
    lane = lax.broadcasted_iota(jnp.int32, (PANEL, LANES), 1)

    def block(k, carry):
        first = pl.multiple_of(k * PANEL, PANEL)
        panel = a_ref[pl.ds(first, PANEL), :]
        d = pltpu.roll(panel, lax.rem(n - k * PANEL, n), 1)[:, :LANES]
        for g in range(PANEL // 8):
            cols = [
                jnp.broadcast_to(d[:, 8 * g + m : 8 * g + m + 1], (PANEL, LANES))
                for m in range(8)
            ]
            for m in range(8):
                j = 8 * g + m
                c = cols[m]
                p = 1.0 / c[j : j + 1, :]
                for mm in range(m + 1, 8):
                    y = cols[mm][j : j + 1, :] * p
                    cols[mm] = jnp.where(sub == j, y, cols[mm] - c * y)
                y = jnp.where(lane[:1] == j, 1.0, d[j : j + 1, :]) * p
                d = jnp.where(sub == j, y, jnp.where(lane == j, 0.0, d) - c * y)
        y = panel - jnp.where(lc == lr + k * PANEL, 1.0, 0.0)
        t = jnp.dot(d[:, :PANEL], y, precision=EXACT, preferred_element_type=F32)
        inside = (ri == ci) & (ri >= k * PANEL) & (ri < k * PANEL + PANEL)
        a_ref[...] = (
            a_ref[...]
            - lax.dot_general(y, t, TN, precision=EXACT, preferred_element_type=F32)
            - jnp.where(inside, 2.0, 0.0)
        )
        return carry

    lax.fori_loop(0, n // PANEL, block, 0)
    a_ref[...] = -a_ref[...] * s_row * s_col


def level(x):
    top = jnp.maximum(jnp.max(jnp.abs(x), axis=0, keepdims=True), 1e-30)
    return jnp.ceil(jnp.log2(top) - 14.99)


def pack(x, into, n):
    power = level(x)
    whole = jnp.clip(jnp.round(x * jnp.exp2(-power)), -32767.0, 32767.0)
    into[:n, :] = whole.astype(jnp.int32).astype(jnp.int16)
    into[n:, :] = jnp.broadcast_to(power, (TILE, x.shape[1])).astype(jnp.int32).astype(jnp.int16)


def unpack(ref, n):
    power = ref[n:, :].astype(jnp.int32).astype(F32)[:1]
    return ref[:n, :].astype(jnp.int32).astype(F32) * jnp.exp2(power)


def kernel(
    nu, ni,
    alpha_ref, u_in, i_in, counts_hbm, u_out, i_out,
    counts, ut, it, un, inat, cf,
    keep, sib_send, sib_recv, rs1_send, rs1_recv, gi_part, gi_recv, gi,
    uh, uht, u_new,
    gu_part, gu_recv, gu,
    rs2_send, rs2_recv, i_new,
    counts_sem, item_send, item_recv, line_send, line_recv, sib_sem, sib_done, user_send, user_recv,
):
    mu, mi = lax.axis_index("user"), lax.axis_index("item")
    d, users = ut.shape
    items = it.shape[1]
    nk = ni // 2
    place, core = mi // 2, lax.rem(mi, 2)
    sibling = mi + 1 - 2 * core
    wu, wi = d // ni, d // nu
    own_u, own_i = users // ni, items // nu
    pair_u, pair_i = 2 * own_u, 2 * own_i
    i_pairs = nu // 2

    def rows(n, k):
        return pl.ds(pl.multiple_of(k * n, n), n)

    def item_peer(off):
        return lax.rem(mi + off, ni)

    def user_peer(off):
        return lax.rem(mu + off, nu)

    def after(off):
        return lax.rem(place + off, nk)

    def before(off):
        return lax.rem(place + nk - off, nk)

    def copy(src, dst, sent, landed, device):
        return pltpu.make_async_remote_copy(
            src_ref=src, dst_ref=dst, send_sem=sent, recv_sem=landed,
            device_id=device, device_id_type=MESH,
        )

    def over_item(kind, off, src, dst):
        return copy(src, dst, item_send.at[kind, off], item_recv.at[kind, off], (mu, item_peer(off)))

    def over_line(kind, off, src, dst):
        return copy(src, dst, line_send.at[kind, off], line_recv.at[kind, off], (mu, 2 * after(off) + core))

    def over_chip(kind, k, src, dst):
        return copy(src, dst, sib_sem.at[kind, k], sib_done.at[kind, k], (mu, sibling))

    def over_user(kind, off, src, dst):
        return copy(src, dst, user_send.at[kind, off], user_recv.at[kind, off], (user_peer(off), mi))

    def ag_user(off, k):
        return over_line(0, off, u_in, ut.at[rows(wu, 2 * k + core), :])

    def ag_user_own():
        return over_chip(0, place, u_in, ut.at[rows(wu, mi), :])

    def ag_user_on(k, c):
        part = ut.at[rows(wu, 2 * k + c), :]
        return over_chip(0, k, part, part)

    def rs1(off):
        return over_line(1, off, rs1_send.at[after(off)], rs1_recv.at[off])

    def halves(k):
        return over_chip(1, k, sib_send.at[k], sib_recv.at[k])

    def gi_rs(off):
        return over_item(0, off, gi_part.at[rows(wu, item_peer(off)), :], gi_recv.at[off])

    def gi_ag(off, who):
        return over_item(1, off, gi.at[rows(wu, who), :], gi.at[rows(wu, who), :])

    def ag_half(off, k):
        part = uh.at[rows(own_u, 2 * k + core), :]
        return over_line(2, off, part, part)

    def ag_half_on(k, c):
        part = uh.at[rows(own_u, 2 * k + c), :]
        return over_chip(2, k, part, part)

    def out_user(off, who):
        return over_item(
            2, off, u_new.at[rows(wu, item_peer(off)), :], u_out.at[:, rows(own_u, who)]
        )

    def ag_item(off, who):
        return over_user(0, off, i_in, it.at[rows(wi, who), :])

    def rs2(off):
        return over_user(1, off, rs2_send.at[user_peer(off)], rs2_recv.at[off])

    def gu_rs(off):
        return over_user(2, off, gu_part.at[rows(wi, user_peer(off)), :], gu_recv.at[off])

    def gu_ag(off, who):
        return over_user(3, off, gu.at[rows(wi, who), :], gu.at[rows(wi, who), :])

    def out_item(off, who):
        return over_user(4, off, i_new.at[rows(wi, user_peer(off)), :], i_out.at[who])

    def each(n, what, first=1):
        def step(off, carry):
            what(off)
            return carry

        lax.fori_loop(first, n, step, 0)

    def from_item(off):
        return lax.rem(mi + ni - off, ni)

    def from_user(off):
        return lax.rem(mu + nu - off, nu)

    def counts_copy(k):
        part = rows(pair_u, k)
        return pltpu.make_async_copy(
            counts_hbm.at[part, :], counts.at[part, :], counts_sem.at[k]
        )

    for k in range(nk):
        counts_copy(k).start()

    barrier = pltpu.get_barrier_semaphore()
    each(ni, lambda off: pl.semaphore_signal(barrier, inc=1, device_id=(mu, item_peer(off)), device_id_type=MESH))
    each(nu, lambda off: pl.semaphore_signal(barrier, inc=1, device_id=(user_peer(off), mi), device_id_type=MESH))
    pl.semaphore_wait(barrier, ni + nu - 2)

    each(nu, lambda off: ag_item(off, mu).start())
    ag_user_own().start()
    each(nk, lambda off: ag_user(off, place).start())
    it[rows(wi, mu), :] = i_in[...]
    ut[rows(wu, mi), :] = u_in[...]

    each(nu, lambda off: ag_item(off, from_user(off)).wait_recv())
    inat[...] = it[...].T
    gi_part[...] = jnp.dot(it[...], inat[...], preferred_element_type=F32)
    each(ni, lambda off: gi_rs(off).start())

    def user_arrived(off):
        ag_user(off, before(off)).wait_recv()
        ag_user_on(before(off), core).start()

    each(nk, user_arrived)
    each(nk, lambda k: ag_user_on(k, 1 - core).wait_recv(), 0)
    un[...] = ut[...].T * jnp.asarray(0.5, BF16)
    for k in range(nk):
        counts_copy(k).wait()

    half_scale = alpha_ref[0] * 0.5

    def coefficients(half_left, part, into):
        step = 256
        for t in range(items // step):
            cols = slice(t * step, (t + 1) * step)
            s = jnp.dot(half_left, it[:, cols], preferred_element_type=F32)
            a = counts[part, cols].astype(F32) * half_scale
            cf[into, cols] = ((a - 0.5) - (a + 0.5) * jnp.tanh(s)).astype(BF16)

    def user_pair(k):
        part = rows(pair_u, k)
        coefficients(un[part, :], part, part)
        grad = jnp.dot(cf[part, :], inat[...], preferred_element_type=F32)
        lower, upper = grad[:own_u], grad[own_u:]
        keep[k] = jnp.where(core == 0, lower, upper)
        sib_send[k] = jnp.where(core == 0, upper, lower)
        halves(k).start()

    def on_to_owner(off):
        k = after(off)
        halves(k).wait_recv()
        pack(keep[k] + sib_recv[k], rs1_send.at[k], own_u)
        rs1(off).start()

    def first_pass(off, carry):
        user_pair(after(off))
        on_to_owner(off - 1)
        return carry

    user_pair(after(1))
    lax.fori_loop(2, 4, first_pass, 0)

    mine = rows(wu, mi)
    each(ni, lambda off: gi_rs(off).wait_recv())
    total = gi_part[mine, :]
    for off in range(1, ni):
        total += gi_recv[off]
    gi[mine, :] = total
    each(ni, lambda off: gi_ag(off, mi).start())

    lax.fori_loop(4, nk, first_pass, 0)
    user_pair(place)
    on_to_owner(nk - 1)

    each(ni, lambda off: gi_ag(off, from_item(off)).wait_recv())
    each(ni, lambda off: gi_rs(off).wait_send())
    gi_part[...] = 0.25 * gi[...] + jnp.where(eye(d), REG, 0.0)
    invert(gi_part)

    halves(place).wait_recv()
    grad = keep[place] + sib_recv[place]
    each(nk, lambda off: rs1(off).wait_recv())
    for off in range(1, nk):
        grad += unpack(rs1_recv.at[off], own_u)
    own = un[rows(own_u, mi), :].astype(F32) * 2.0
    grad = grad - REG * own
    new = own + jnp.dot(grad, gi_part[...], precision=EXACT, preferred_element_type=F32)
    uh[rows(own_u, mi), :] = new.astype(BF16)
    ag_half_on(place, core).start()
    each(nk, lambda off: ag_half(off, place).start())
    u_new[...] = new.T
    u_out[:, rows(own_u, mi)] = u_new[mine, :]
    each(ni, lambda off: out_user(off, mi).start())

    def half_arrived(off):
        ag_half(off, before(off)).wait_recv()
        ag_half_on(before(off), core).start()

    def second_pass(k):
        ag_half_on(k, 1 - core).wait_recv()
        part = rows(pair_u, k)
        half = uh[part, :]
        uht[:, part] = half.T
        coefficients(half * jnp.asarray(0.5, BF16), part, part)

    def second_step(off, carry):
        half_arrived(off + 1)
        second_pass(before(off))
        return carry

    lax.fori_loop(0, nk - 1, second_step, 0)
    second_pass(before(nk - 1))

    gu_part[...] = jnp.dot(uht[...], uh[...], preferred_element_type=F32)
    each(nu, lambda off: gu_rs(off).start())

    def item_pair(q, carry):
        g = jnp.dot(uht[...], cf[:, rows(pair_i, q)], preferred_element_type=F32)
        g = g.T
        pack(g[:own_i], rs2_send.at[2 * q], own_i)
        pack(g[own_i:], rs2_send.at[2 * q + 1], own_i)
        return carry

    lax.fori_loop(0, i_pairs, item_pair, 0)

    slab = rows(wi, mu)
    each(nu, lambda off: gu_rs(off).wait_recv())
    total = gu_part[slab, :]
    for off in range(1, nu):
        total += gu_recv[off]
    gu[slab, :] = total
    each(nu, lambda off: gu_ag(off, mu).start())
    each(nu, lambda off: rs2(off).start())
    each(nu, lambda off: gu_ag(off, from_user(off)).wait_recv())
    each(nu, lambda off: gu_rs(off).wait_send())
    gu_part[...] = 0.25 * gu[...] + jnp.where(eye(d), REG, 0.0)
    invert(gu_part)

    grad = unpack(rs2_send.at[mu], own_i)
    each(nu, lambda off: rs2(off).wait_recv())
    for off in range(1, nu):
        grad += unpack(rs2_recv.at[off], own_i)
    own = inat[rows(own_i, mu), :].astype(F32)
    grad = grad - REG * own
    new = own + jnp.dot(grad, gu_part[...], precision=EXACT, preferred_element_type=F32)
    i_new[...] = new.T
    each(nu, lambda off: out_item(off, mu).start())
    i_out[mu] = i_new[slab, :]

    each(ni, lambda off: out_user(off, from_item(off)).wait_recv())
    each(nu, lambda off: out_item(off, from_user(off)).wait_recv())

    def drain_item(off):
        gi_ag(off, mi).wait_send()
        out_user(off, mi).wait_send()

    def drain_line(off):
        ag_user(off, place).wait_send()
        rs1(off).wait_send()
        ag_half(off, place).wait_send()

    def drain_chip(k):
        ag_user_on(k, core).wait_send()
        halves(k).wait_send()
        ag_half_on(k, core).wait_send()

    def drain_user(off):
        ag_item(off, mu).wait_send()
        rs2(off).wait_send()
        gu_ag(off, mu).wait_send()
        out_item(off, mu).wait_send()

    each(ni, drain_item)
    each(nk, drain_line)
    each(nk, drain_chip, 0)
    each(nu, drain_user)


def on_device(nu, ni, counts, user_factors, item_factors, alpha_scale):
    users, items = counts.shape
    d = user_factors.shape[1] * ni
    nk = ni // 2
    wu, wi, own_u, own_i = d // ni, d // nu, users // ni, items // nu
    vmem = pl.BlockSpec(memory_space=pltpu.VMEM)
    spare, dma = pltpu.VMEM, pltpu.SemaphoreType.DMA
    u_out, i_out = pl.pallas_call(
        functools.partial(kernel, nu, ni),
        out_shape=(
            jax.ShapeDtypeStruct((wu, users), F32),
            jax.ShapeDtypeStruct((nu, wi, own_i), F32),
        ),
        in_specs=[
            pl.BlockSpec(memory_space=pltpu.SMEM), vmem, vmem, pl.BlockSpec(memory_space=pl.ANY),
        ],
        out_specs=(vmem, vmem),
        scratch_shapes=[
            spare((users, items), jnp.int32),
            spare((d, users), BF16), spare((d, items), BF16),
            spare((users, d), BF16), spare((items, d), BF16),
            spare((users, items), BF16),
            spare((nk, own_u, d), F32), spare((nk, own_u, d), F32), spare((nk, own_u, d), F32),
            spare((nk, own_u + TILE, d), jnp.int16), spare((nk, own_u + TILE, d), jnp.int16),
            spare((d, d), F32), spare((ni, wu, d), F32), spare((d, d), F32),
            spare((users, d), BF16), spare((d, users), BF16), spare((d, own_u), F32),
            spare((d, d), F32), spare((nu, wi, d), F32), spare((d, d), F32),
            spare((nu, own_i + TILE, d), jnp.int16), spare((nu, own_i + TILE, d), jnp.int16),
            spare((d, own_i), F32),
            dma((nk,)), dma((3, ni)), dma((3, ni)), dma((3, nk)), dma((3, nk)),
            dma((3, nk)), dma((3, nk)), dma((5, nu)), dma((5, nu)),
        ],
        compiler_params=pltpu.CompilerParams(
            collective_id=0, has_side_effects=True, vmem_limit_bytes=60 << 20
        ),
    )(alpha_scale, user_factors.T, item_factors.T, counts)
    return u_out.T, i_out.transpose(0, 2, 1).reshape(items, wi)


def solution(mesh):
    in_specs = (P("user", "item"), P("user", "item"), P("item", "user"), P())
    out_specs = (P("user", "item"), P("item", "user"))
    return jax.shard_map(
        functools.partial(on_device, mesh.shape["user"], mesh.shape["item"]),
        mesh=mesh, in_specs=in_specs, out_specs=out_specs, check_vma=False,
    )
```

time: 458 us -> 105 us (0.23); the launches traced: 453 us -> 105 us
  waiting for transfers between devices: 224 us -> 0 us
  other arithmetic: 117 us -> 0 us
  Pallas kernels: 0 us -> 100 us
  matrix products: 40.4 us -> 0 us
  blocking collectives: 36.5 us -> 0 us
  between operations: 17.5 us -> 1.29 us
  local copies, waits for them, and re-layouts: 17.1 us -> 3.47 us
    psum x2 -> x0, waiting for transfers between devices: 223 us -> none  [the longest x1 124 us: on_device(): lax.psum(jnp.dot(coefficient, item_full, preferred_element_type=jnp.float...]
    another operation x18 -> x0, other arithmetic: 109 us -> none  [the longest x13 68.9 us: newton(): factor_low = jnp.linalg.cholesky(bound)]
    pallas_call x0 -> x1, Pallas kernels: none -> 100 us  [on_device(): pl.pallas_call(functools.partial(kernel, nu, ni), out_shape=(jax.ShapeDty...]
    all_gather x1 -> x0, blocking collectives: 36.5 us -> none  [on_device(): item_full = lax.all_gather(item_factors, 'user', axis=1, tiled=True)]
    dot_general x4 -> x0, matrix products: 25.4 us -> none  [the longest x1 12.1 us: on_device(): jnp.einsum('ui,ud->id', coefficient_next, user_half, preferred_element_ty...]
    another operation x16 -> x0, matrix products: 14.9 us -> none  [the longest x12 14 us: newton(): return jax.scipy.linalg.cho_solve((factor_low, True), gradient.T).T]
    another operation x19 -> x0, local copies, waits for them, and re-layouts: 9.67 us -> none
  transfers between devices with their start and end apart: 3 -> 0, of which waited for: 3 -> 0; matrix products, arithmetic and copies ran while one was open for 2% -> 0% of each run, Pallas kernels for 0% -> 0%
where the time goes in v1:
time: 105 us
  Pallas kernels  100 us (95%)
  local copies, waits for them, and re-layouts  3.47 us (3%)
  between operations  1.29 us (1%)
    pallas_call x1, Pallas kernels, on_device(): pl.pallas_call(functools.partial(kernel, nu, ni), out_shape=(jax.ShapeDty...  100 us

profile of v1, /device:TPU:0, one launch (start us, length us, event | category | flops | bytes accessed | tf_op | source)
XLA Modules:
  0.0 105.0 jit_solution(8924108213310925532)
XLA Ops:
  1.3 100.3 %shard_map.59 = (f32[16,2048]{1,0:T(8,128)}, f32[8,32,192]{2,1,0:T(8,128)}) custom-call(f32[1]{0:T(128)S(6)} %copy.8.alpha_ref, bf16[16,2048]{1,0:T(8,128)(2,1)} %bitcast.9, bf16[32,1536]{1,0:T(8,128)(2,1)} %bitcast.8, s32[2048,1536]{1,0:T(8,128)} %counts_hbm.1), custom_call_target="tpu_custom_call" | custom-call | tf_op jit(solution)/shard_map/pallas_call | solution.py:398
  101.6 1.1 %copy.6 = f32[8,192,32]{1,0,2:T(8,128)S(1)} copy(f32[8,192,32]{1,2,0:T(8,128)} %bitcast.6) | data formatting | bytes 393216 | tf_op jit(solution)/shard_map/transpose | solution.py:427
  102.7 0.8 reshape.7
  103.5 1.6 %copy.9 = f32[2048,16]{0,1:T(8,128)} copy(f32[2048,16]{0,1:T(8,128)} %bitcast.7) | data formatting | bytes 262144

commit v2 on v1

v2 whole, which is shorter than its diff:
```python
import functools

import jax
import jax.numpy as jnp
from jax import lax
from jax.experimental import pallas as pl
from jax.experimental.pallas import tpu as pltpu
from jax.sharding import PartitionSpec as P

MESH = pl.DeviceIdType.MESH
EXACT = lax.Precision.HIGHEST
F32 = jnp.float32
BF16 = jnp.bfloat16
TN = (((0,), (0,)), ((), ()))
NT = (((1,), (1,)), ((), ()))
REG = 1.0
PANEL = 32
LANES = 128
TILE = 16
STEPS_BESIDE = 6
HOPS = (
    (1, 0, 0, 0, None, None),
    (-1, 0, 0, 0, None, None),
    (0, 1, 0, 0, None, None),
    (1, 0, -1, 0, 0, 0),
    (-1, 0, 1, 0, 1, 1),
    (1, 1, -1, 0, 0, 0),
    (-1, 1, 1, 0, 1, 1),
    (1, 0, 0, 1, None, 2),
    (-1, 0, 0, 1, None, 2),
)


def eye(n):
    return lax.broadcasted_iota(jnp.int32, (n, n), 0) == lax.broadcasted_iota(
        jnp.int32, (n, n), 1
    )


def scales(h):
    diagonal = jnp.where(eye(h.shape[0]), h, 0.0)
    return (
        lax.rsqrt(jnp.sum(diagonal, axis=0, keepdims=True)),
        lax.rsqrt(jnp.sum(diagonal, axis=1, keepdims=True)),
    )


def eliminations(d):
    sub = lax.broadcasted_iota(jnp.int32, (PANEL, LANES), 0)
    lane = lax.broadcasted_iota(jnp.int32, (PANEL, LANES), 1)

    def step(j):
        m = j % 8
        now = d["now"]
        if m == 0:
            d["cols"] = [jnp.broadcast_to(now[:, j + q : j + q + 1], (PANEL, LANES)) for q in range(8)]
        cols = d["cols"]
        c = cols[m]
        p = 1.0 / c[j : j + 1, :]
        for mm in range(m + 1, 8):
            y = cols[mm][j : j + 1, :] * p
            cols[mm] = jnp.where(sub == j, y, cols[mm] - c * y)
        y = jnp.where(lane[:1] == j, 1.0, now[j : j + 1, :]) * p
        d["now"] = jnp.where(sub == j, y, jnp.where(lane == j, 0.0, now) - c * y)

    return [functools.partial(step, j) for j in range(PANEL)]


class Sweep:
    def __init__(self, a_ref, u_ref, y_ref):
        self.a, self.u, self.y = a_ref, u_ref, y_ref
        self.n = a_ref.shape[0]

    def begin(self, h):
        s_row, s_col = scales(h)
        self.a[...] = h * s_row * s_col
        self.u[...] = jnp.zeros_like(self.u)
        self.y[...] = jnp.zeros_like(self.y)

    def update(self, k):
        ri = lax.broadcasted_iota(jnp.int32, (self.n, self.n), 0)
        inside = eye(self.n) & (ri >= (k - 1) * PANEL) & (ri < k * PANEL)
        return jnp.dot(self.u[:, :PANEL], self.y[...], precision=EXACT, preferred_element_type=F32) + jnp.where(inside, 2.0, 0.0)

    def block(self, k, beside=()):
        n = self.n
        rows = pl.ds(pl.multiple_of(k * PANEL, PANEL), PANEL)
        panel = self.a[rows, :] - jnp.dot(self.u[rows, :PANEL], self.y[...], precision=EXACT, preferred_element_type=F32)
        d = {"now": pltpu.roll(panel, lax.rem(n - k * PANEL, n), 1)[:, :LANES]}
        steps = eliminations(d)
        for work in beside[:-1]:
            work()
            for _ in range(STEPS_BESIDE):
                if steps:
                    steps.pop(0)()
        for step in steps:
            step()
        for work in beside[-1:]:
            work()
        self.a[...] = self.a[...] - self.update(k)
        lr = lax.broadcasted_iota(jnp.int32, (PANEL, n), 0)
        lc = lax.broadcasted_iota(jnp.int32, (PANEL, n), 1)
        y = panel - jnp.where(lc == lr + k * PANEL, 1.0, 0.0)
        self.y[...] = y
        self.u[:, :PANEL] = lax.dot_general(y, d["now"][:, :PANEL], TN, precision=EXACT, preferred_element_type=F32)

    def end(self, h):
        s_row, s_col = scales(h)
        self.a[...] = (self.update(self.n // PANEL) - self.a[...]) * s_row * s_col


def level(x):
    top = jnp.maximum(jnp.max(jnp.abs(x), axis=0, keepdims=True), 1e-30)
    return jnp.ceil(jnp.log2(top) - 14.99)


def pack(x, into, n):
    power = level(x)
    whole = jnp.clip(jnp.round(x * jnp.exp2(-power)), -32767.0, 32767.0)
    into[:n, :] = whole.astype(jnp.int32).astype(jnp.int16)
    into[n:, :] = jnp.broadcast_to(power, (TILE, x.shape[1])).astype(jnp.int32).astype(jnp.int16)


def unpack(ref, n):
    power = ref[n:, :].astype(jnp.int32).astype(F32)[:1]
    return ref[:n, :].astype(jnp.int32).astype(F32) * jnp.exp2(power)


def kernel(
    nu, ni,
    alpha_ref, u_in, i_in, counts_hbm, u_out, i_out,
    counts, ut, it, inat, cf,
    keep, sib_send, sib_recv, rs1_send, rs1_recv, gi_part, gi_recv, gi,
    uh, uht, u_new,
    gu_rows, gu,
    rs2_send, rs2_recv, i_new,
    inv_a, inv_u, inv_y,
    counts_sem, item_send, item_recv, line_send, line_recv, sib_sem, sib_done, user_send, user_recv,
    ring_send, ring_recv,
):
    mu, mi = lax.axis_index("user"), lax.axis_index("item")
    d, users = ut.shape
    items = it.shape[1]
    nk = ni // 2
    place, core = mi // 2, lax.rem(mi, 2)
    sibling = mi + 1 - 2 * core
    wu, wi = d // ni, d // nu
    own_u, own_i = users // ni, items // nu
    pair_u, pair_i = 2 * own_u, 2 * own_i
    i_pairs = nu // 2

    def rows(n, k):
        return pl.ds(pl.multiple_of(k * n, n), n)

    def item_peer(off):
        return lax.rem(mi + off, ni)

    def user_peer(off):
        return lax.rem(mu + off, nu)

    def after(off):
        return lax.rem(place + off, nk)

    def chip_at(along, across):
        y, z = lax.rem(place, 4), place // 4
        return 4 * lax.rem(z + across + 2, 2) + lax.rem(y + along + 4, 4)

    def group_at(along, across):
        x, z = mu // 2, lax.rem(mu, 2)
        return 2 * lax.rem(x + along + 4, 4) + lax.rem(z + across + 2, 2)

    def copy(src, dst, sent, landed, device):
        return pltpu.make_async_remote_copy(
            src_ref=src, dst_ref=dst, send_sem=sent, recv_sem=landed,
            device_id=device, device_id_type=MESH,
        )

    def over_item(kind, off, src, dst):
        return copy(src, dst, item_send.at[kind, off], item_recv.at[kind, off], (mu, item_peer(off)))

    def over_line(kind, off, src, dst):
        return copy(src, dst, line_send.at[kind, off], line_recv.at[kind, off], (mu, 2 * after(off) + core))

    def over_chip(kind, k, src, dst):
        return copy(src, dst, sib_sem.at[kind, k], sib_done.at[kind, k], (mu, sibling))

    def over_user(kind, off, src, dst):
        return copy(src, dst, user_send.at[kind, off], user_recv.at[kind, off], (user_peer(off), mi))

    class Gather:
        def __init__(self, kind, at, to, part):
            self.kind, self.at, self.to, self.part = kind, at, to, part

        def hop(self, slot):
            along, across, b_along, b_across, half, _ = HOPS[slot]
            ref = self.part(self.at(b_along, b_across), half)
            return copy(ref, ref, ring_send.at[self.kind, slot], ring_recv.at[self.kind, slot], self.to(self.at(along, across)))

        def landed(self, slot):
            along, across, b_along, b_across, half, _ = HOPS[slot]
            return self.part(self.at(b_along - along, b_across - across), half)

        def start(self):
            for slot in range(3):
                self.hop(slot).start()

        def arrived(self, slot):
            ref = self.landed(slot)
            copy(ref, ref, ring_send.at[self.kind, slot], ring_recv.at[self.kind, slot], self.to(self.at(0, 1))).wait_recv()
            for later in range(len(HOPS)):
                if HOPS[later][-1] == slot:
                    self.hop(later).start()

        def drain(self):
            for slot in range(len(HOPS)):
                self.hop(slot).wait_send()

    def item_part(k, half):
        if half is None:
            return it.at[rows(wi, k), :]
        return it.at[rows(wi // 2, 2 * k + half), :]

    def user_part_of(c):
        def part(k, half):
            if half is None:
                return ut.at[rows(wu, 2 * k + c), :]
            return ut.at[rows(wu, 2 * k + c), pl.ds(half * (users // 2), users // 2)]

        return part

    def half_part_of(c):
        def part(k, half):
            if half is None:
                return uh.at[rows(own_u, 2 * k + c), :]
            return uh.at[rows(own_u // 2, 4 * k + 2 * c + half), :]

        return part

    def same_core(k):
        return (mu, 2 * k + core)

    gather_items = Gather(0, group_at, lambda k: (k, mi), item_part)
    gather_users = Gather(1, chip_at, same_core, user_part_of(core))
    gather_half = Gather(2, chip_at, same_core, half_part_of(core))

    def passed_on(kind, slot, part_of, c):
        if slot == len(HOPS):
            ref = part_of(c)(place, None)
        else:
            along, across, b_along, b_across, half, _ = HOPS[slot]
            ref = part_of(c)(chip_at(b_along - along, b_across - across), half)
        return over_chip(kind, slot, ref, ref)

    def user_on(slot, c):
        return passed_on(0, slot, user_part_of, c)

    def half_on(slot, c):
        return passed_on(1, slot, half_part_of, c)

    own_slot = len(HOPS)

    def halves(k):
        return over_chip(2, k, sib_send.at[k], sib_recv.at[k])

    def rs1(off):
        return over_line(0, off, rs1_send.at[after(off)], rs1_recv.at[off])

    def gi_rs(off):
        return over_item(0, off, gi_part.at[rows(wu, item_peer(off)), :], gi_recv.at[off])

    def gi_ag(off, who):
        return over_item(1, off, gi.at[rows(wu, who), :], gi.at[rows(wu, who), :])

    def out_user(off, who):
        return over_item(
            2, off, u_new.at[rows(wu, item_peer(off)), :], u_out.at[:, rows(own_u, who)]
        )

    def gu_ag(off, who):
        return over_item(3, off, gu.at[rows(wu, who), :], gu.at[rows(wu, who), :])

    def rs2(off):
        return over_user(0, off, rs2_send.at[user_peer(off)], rs2_recv.at[off])

    def gu_rs(off, who):
        return over_user(1, off, gu_rows.at[who], gu_rows.at[who])

    def out_item(off, who):
        return over_user(2, off, i_new.at[rows(wi, user_peer(off)), :], i_out.at[who])

    def each(n, what, first=1):
        def step(off, carry):
            what(off)
            return carry

        lax.fori_loop(first, n, step, 0)

    def from_item(off):
        return lax.rem(mi + ni - off, ni)

    def from_user(off):
        return lax.rem(mu + nu - off, nu)

    def counts_copy(k):
        part = rows(pair_u, k)
        return pltpu.make_async_copy(
            counts_hbm.at[part, :], counts.at[part, :], counts_sem.at[k]
        )

    for k in range(nk):
        counts_copy(k).start()
    it[rows(wi, mu), :] = i_in[...]
    ut[rows(wu, mi), :] = u_in[...]

    barrier = pltpu.get_barrier_semaphore()
    each(ni, lambda off: pl.semaphore_signal(barrier, inc=1, device_id=(mu, item_peer(off)), device_id_type=MESH))
    each(nu, lambda off: pl.semaphore_signal(barrier, inc=1, device_id=(user_peer(off), mi), device_id_type=MESH))
    pl.semaphore_wait(barrier, ni + nu - 2)

    gather_items.start()
    gather_users.start()
    user_on(own_slot, core).start()
    for slot in range(2):
        gather_items.arrived(slot)
    for slot in range(2):
        gather_users.arrived(slot)
        user_on(slot, core).start()
    gather_items.arrived(2)
    gather_users.arrived(2)
    user_on(2, core).start()
    for slot in range(3, len(HOPS)):
        gather_items.arrived(slot)

    gi_part[...] = lax.dot_general(it[...], it[...], NT, preferred_element_type=F32)
    each(ni, lambda off: gi_rs(off).start())
    inat[...] = it[...].T

    for slot in range(3, len(HOPS)):
        gather_users.arrived(slot)
        user_on(slot, core).start()
    mine = rows(wu, mi)
    each(ni, lambda off: gi_rs(off).wait_recv())
    total = gi_part[mine, :]
    for off in range(1, ni):
        total += gi_recv[off]
    gi[mine, :] = total
    each(ni, lambda off: gi_ag(off, mi).start())

    for slot in range(len(HOPS) + 1):
        user_on(slot, 1 - core).wait_recv()
    for k in range(nk):
        counts_copy(k).wait()

    half_scale = alpha_ref[0] * 0.5

    def coefficients(half_left, part):
        step = 256

        def tile(t):
            cols = slice(t * step, (t + 1) * step)
            s = jnp.dot(half_left, it[:, cols], preferred_element_type=F32)
            a = counts[part, cols].astype(F32) * half_scale
            cf[part, cols] = ((a - 0.5) - (a + 0.5) * jnp.tanh(s)).astype(BF16)

        return [functools.partial(tile, t) for t in range(items // step)]

    def user_pair(k):
        part = rows(pair_u, k)

        def gradient():
            grad = jnp.dot(cf[part, :], inat[...], preferred_element_type=F32)
            lower, upper = grad[:own_u], grad[own_u:]
            keep[k] = jnp.where(core == 0, lower, upper)
            sib_send[k] = jnp.where(core == 0, upper, lower)

        return coefficients(ut[:, part].T * jnp.asarray(0.5, BF16), part) + [gradient]

    def on_to_owner(off):
        k = after(off)
        halves(k).wait_recv()
        pack(keep[k] + sib_recv[k], rs1_send.at[k], own_u)
        rs1(off).start()

    sweep = Sweep(inv_a, inv_u, inv_y)
    for work in user_pair(after(1)):
        work()
    halves(after(1)).start()
    each(ni, lambda off: gi_ag(off, from_item(off)).wait_recv())

    def hessian(gram):
        return 0.25 * gram[...] + jnp.where(eye(d), REG, 0.0)

    sweep.begin(hessian(gi))

    def first_pass(off, carry):
        sweep.block(off - 2, user_pair(after(off)))
        halves(after(off)).start()
        on_to_owner(off - 1)
        return carry

    lax.fori_loop(2, nk + 1, first_pass, 0)
    sweep.block(nk - 1)
    sweep.end(hessian(gi))

    halves(place).wait_recv()
    grad = keep[place] + sib_recv[place]
    each(nk, lambda off: rs1(off).wait_recv())
    for off in range(1, nk):
        grad += unpack(rs1_recv.at[off], own_u)
    own = ut[:, rows(own_u, mi)].T.astype(F32)
    grad = grad - REG * own
    new = own + jnp.dot(grad, inv_a[...], precision=EXACT, preferred_element_type=F32)
    uh[rows(own_u, mi), :] = new.astype(BF16)
    gather_half.start()
    half_on(own_slot, core).start()
    u_new[...] = new.T
    u_out[:, rows(own_u, mi)] = u_new[mine, :]

    def turn(k):
        part = rows(pair_u, k)
        uht[:, part] = uh[part, :].T

    def second_pass(k):
        part = rows(pair_u, k)
        half = uh[part, :]
        for work in coefficients(half * jnp.asarray(0.5, BF16), part):
            work()

    half_on(own_slot, 1 - core).wait_recv()
    second_pass(place)
    turn(place)
    for slot in range(3):
        gather_half.arrived(slot)
        half_on(slot, core).start()
    for slot in range(3):
        half_on(slot, 1 - core).wait_recv()

    def near(t, carry):
        k = chip_at(jnp.where(t == 0, -1, jnp.where(t == 1, 1, 0)), jnp.where(t == 2, 1, 0))
        second_pass(k)
        turn(k)
        return carry

    lax.fori_loop(0, 3, near, 0)
    for slot in range(3, len(HOPS)):
        gather_half.arrived(slot)
        half_on(slot, core).start()
    for slot in range(3, len(HOPS)):
        half_on(slot, 1 - core).wait_recv()

    def far(t):
        return chip_at(jnp.where(t < 2, 2, jnp.where(t == 2, 1, -1)), jnp.where(t == 0, 0, 1))

    def far_turn(t, carry):
        turn(far(t))
        return carry

    def far_pass(t, carry):
        second_pass(far(t))
        return carry

    lax.fori_loop(0, 4, far_turn, 0)
    gu_rows[mu] = jnp.dot(uht[mine, :], uh[...], preferred_element_type=F32)
    each(nu, lambda off: gu_rs(off, mu).start())
    lax.fori_loop(0, 4, far_pass, 0)
    each(nu, lambda off: gu_rs(off, from_user(off)).wait_recv())
    total = gu_rows[0]
    for k in range(1, nu):
        total += gu_rows[k]
    gu[mine, :] = total
    each(ni, lambda off: gu_ag(off, mi).start())

    def item_pair(q):
        g = jnp.dot(uht[...], cf[:, rows(pair_i, q)], preferred_element_type=F32)
        g = g.T
        pack(g[:own_i], rs2_send.at[2 * q], own_i)
        pack(g[own_i:], rs2_send.at[2 * q + 1], own_i)

    def item_step(q, carry):
        item_pair(q)
        return carry

    lax.fori_loop(0, i_pairs, item_step, 0)
    each(ni, lambda off: gu_ag(off, from_item(off)).wait_recv())
    each(nu, lambda off: rs2(off).start())
    each(ni, lambda off: out_user(off, mi).start())
    sweep.begin(hessian(gu))

    def sweep_on(k, carry):
        sweep.block(k)
        return carry

    lax.fori_loop(0, d // PANEL, sweep_on, 0)
    sweep.end(hessian(gu))

    grad = unpack(rs2_send.at[mu], own_i)
    each(nu, lambda off: rs2(off).wait_recv())
    for off in range(1, nu):
        grad += unpack(rs2_recv.at[off], own_i)
    own = inat[rows(own_i, mu), :].astype(F32)
    grad = grad - REG * own
    new = own + jnp.dot(grad, inv_a[...], precision=EXACT, preferred_element_type=F32)
    i_new[...] = new.T
    each(nu, lambda off: out_item(off, mu).start())
    i_out[mu] = i_new[rows(wi, mu), :]

    gather_items.drain()
    gather_users.drain()
    gather_half.drain()

    def drain_item(off):
        gi_rs(off).wait_send()
        gi_ag(off, mi).wait_send()
        gu_ag(off, mi).wait_send()
        out_user(off, mi).wait_send()

    def drain_chip(k):
        halves(k).wait_send()

    def drain_user(off):
        rs2(off).wait_send()
        gu_rs(off, mu).wait_send()

    each(ni, drain_item)
    each(nk, lambda off: rs1(off).wait_send())
    each(nk, drain_chip, 0)
    for slot in range(len(HOPS) + 1):
        user_on(slot, core).wait_send()
        half_on(slot, core).wait_send()
    each(nu, drain_user)
    each(ni, lambda off: out_user(off, from_item(off)).wait_recv())
    each(nu, lambda off: out_item(off, from_user(off)).wait_recv())
    each(nu, lambda off: out_item(off, mu).wait_send())


def on_device(nu, ni, counts, user_factors, item_factors, alpha_scale):
    users, items = counts.shape
    d = user_factors.shape[1] * ni
    nk, slots = ni // 2, len(HOPS)
    wu, wi, own_u, own_i = d // ni, d // nu, users // ni, items // nu
    vmem = pl.BlockSpec(memory_space=pltpu.VMEM)
    spare, dma = pltpu.VMEM, pltpu.SemaphoreType.DMA
    u_out, i_out = pl.pallas_call(
        functools.partial(kernel, nu, ni),
        out_shape=(
            jax.ShapeDtypeStruct((wu, users), F32),
            jax.ShapeDtypeStruct((nu, wi, own_i), F32),
        ),
        in_specs=[
            pl.BlockSpec(memory_space=pltpu.SMEM), vmem, vmem, pl.BlockSpec(memory_space=pl.ANY),
        ],
        out_specs=(vmem, vmem),
        scratch_shapes=[
            spare((users, items), jnp.int32),
            spare((d, users), BF16), spare((d, items), BF16),
            spare((items, d), BF16),
            spare((users, items), BF16),
            spare((nk, own_u, d), F32), spare((nk, own_u, d), F32), spare((nk, own_u, d), F32),
            spare((nk, own_u + TILE, d), jnp.int16), spare((nk, own_u + TILE, d), jnp.int16),
            spare((d, d), F32), spare((ni, wu, d), F32), spare((d, d), F32),
            spare((users, d), BF16), spare((d, users), BF16), spare((d, own_u), F32),
            spare((nu, wu, d), F32), spare((d, d), F32),
            spare((nu, own_i + TILE, d), jnp.int16), spare((nu, own_i + TILE, d), jnp.int16),
            spare((d, own_i), F32),
            spare((d, d), F32), spare((d, LANES), F32), spare((PANEL, d), F32),
            dma((nk,)), dma((4, ni)), dma((4, ni)), dma((1, nk)), dma((1, nk)),
            dma((3, slots + 1)), dma((3, slots + 1)), dma((3, nu)), dma((3, nu)),
            dma((3, slots)), dma((3, slots)),
        ],
        compiler_params=pltpu.CompilerParams(
            collective_id=0, has_side_effects=True, vmem_limit_bytes=60 << 20
        ),
    )(alpha_scale, user_factors.T, item_factors.T, counts)

    def lay(u_ref, i_ref, u_to, i_to):
        u_to[...] = u_ref[...]
        for k in range(0, nu, 2):
            pair = jnp.concatenate([i_ref[k], i_ref[k + 1]], axis=1)
            i_to[:, k * own_i : (k + 2) * own_i] = pair

    u_new, i_new = pl.pallas_call(
        lay,
        out_shape=(jax.ShapeDtypeStruct((wu, users), F32), jax.ShapeDtypeStruct((wi, items), F32)),
        in_specs=[vmem, vmem],
        out_specs=(vmem, vmem),
    )(u_out, i_out)
    return u_new.T, i_new.T


def solution(mesh):
    in_specs = (P("user", "item"), P("user", "item"), P("item", "user"), P())
    out_specs = (P("user", "item"), P("item", "user"))
    return jax.shard_map(
        functools.partial(on_device, mesh.shape["user"], mesh.shape["item"]),
        mesh=mesh, in_specs=in_specs, out_specs=out_specs, check_vma=False,
    )
```

time: 105 us -> 95.6 us (0.910)
  Pallas kernels: 100 us -> 94.1 us
  local copies, waits for them, and re-layouts: 3.47 us -> 0 us
    pallas_call x1, Pallas kernels: 100 us -> 92.3 us  [on_device(): pl.pallas_call(functools.partial(kernel, nu, ni), out_shape=(jax.ShapeDty...]
    pallas_call x0 -> x1, Pallas kernels: none -> 1.8 us  [on_device(): pl.pallas_call(lay, out_shape=(jax.ShapeDtypeStruct((wu, users), F32), ja...]
    unnamed x1 -> x0, local copies, waits for them, and re-layouts: 1.57 us -> none
    transpose x1 -> x0, local copies, waits for them, and re-layouts: 1.11 us -> none  [on_device(): return (u_out.T, i_out.transpose(0, 2, 1).reshape(items, wi))]
where the time goes in v2:
time: 95.6 us; the launch traced here: 95.4 us
  Pallas kernels  94.1 us (98%)
  between operations  1.29 us (1%)
    pallas_call x1, Pallas kernels, on_device(): pl.pallas_call(functools.partial(kernel, nu, ni), out_shape=(jax.ShapeDty...  92.3 us

profile of v2, /device:TPU:0, one launch (start us, length us, event | category | flops | bytes accessed | tf_op | source)
XLA Modules:
  0.0 95.4 jit_solution(3899812950968659015)
XLA Ops:
  1.3 92.3 %shard_map.59 = (f32[16,2048]{1,0:T(8,128)}, f32[8,32,192]{2,1,0:T(8,128)}) custom-call(f32[1]{0:T(128)S(6)} %copy.6.alpha_ref, bf16[16,2048]{1,0:T(8,128)(2,1)} %bitcast.5, bf16[32,1536]{1,0:T(8,128)(2,1)} %bitcast.4, s32[2048,1536]{1,0:T(8,128)} %counts_hbm.1), custom_call_target="tpu_custom_call" | custom-call | tf_op jit(solution)/shard_map/pallas_call | solution.py:543
  93.6 1.8 %shard_map.60 = (f32[16,2048]{1,0:T(8,128)}, f32[32,1536]{1,0:T(8,128)}) custom-call(f32[16,2048]{1,0:T(8,128)} %get-tuple-element.6.u_ref, f32[8,32,192]{2,1,0:T(8,128)} %get-tuple-element.7.i_ref), custom_call_target="tpu_custom_call" | custom-call | tf_op jit(solution)/shard_map/pallas_call | solution.py:581

commit v3 on v2

--- a/solution.py
+++ b/solution.py
@@ -404,8 +404,8 @@
 
     halves(place).wait_recv()
     grad = keep[place] + sib_recv[place]
-    each(nk, lambda off: rs1(off).wait_recv())
     for off in range(1, nk):
+        rs1(off).wait_recv()
         grad += unpack(rs1_recv.at[off], own_u)
     own = ut[:, rows(own_u, mi)].T.astype(F32)
     grad = grad - REG * own
@@ -462,6 +462,7 @@
     lax.fori_loop(0, 4, far_turn, 0)
     gu_rows[mu] = jnp.dot(uht[mine, :], uh[...], preferred_element_type=F32)
     each(nu, lambda off: gu_rs(off, mu).start())
+    each(ni, lambda off: out_user(off, mi).start())
     lax.fori_loop(0, 4, far_pass, 0)
     each(nu, lambda off: gu_rs(off, from_user(off)).wait_recv())
     total = gu_rows[0]
@@ -482,8 +483,7 @@
 
     lax.fori_loop(0, i_pairs, item_step, 0)
     each(ni, lambda off: gu_ag(off, from_item(off)).wait_recv())
-    each(nu, lambda off: rs2(off).start())
-    each(ni, lambda off: out_user(off, mi).start())
+    each(nu, lambda off: rs2(nu - off).start())
     sweep.begin(hessian(gu))
 
     def sweep_on(k, carry):
@@ -494,13 +494,13 @@
     sweep.end(hessian(gu))
 
     grad = unpack(rs2_send.at[mu], own_i)
-    each(nu, lambda off: rs2(off).wait_recv())
-    for off in range(1, nu):
+    for off in range(nu - 1, 0, -1):
+        rs2(off).wait_recv()
         grad += unpack(rs2_recv.at[off], own_i)
     own = inat[rows(own_i, mu), :].astype(F32)
     grad = grad - REG * own
     new = own + jnp.dot(grad, inv_a[...], precision=EXACT, preferred_element_type=F32)
-    i_new[...] = new.T
+    i_new[:, :own_i] = new.T
     each(nu, lambda off: out_item(off, mu).start())
     i_out[mu] = i_new[rows(wi, mu), :]
 
@@ -544,7 +544,7 @@
         functools.partial(kernel, nu, ni),
         out_shape=(
             jax.ShapeDtypeStruct((wu, users), F32),
-            jax.ShapeDtypeStruct((nu, wi, own_i), F32),
+            jax.ShapeDtypeStruct((nu, wi, 2 * LANES), F32),
         ),
         in_specs=[
             pl.BlockSpec(memory_space=pltpu.SMEM), vmem, vmem, pl.BlockSpec(memory_space=pl.ANY),
@@ -561,7 +561,7 @@
             spare((users, d), BF16), spare((d, users), BF16), spare((d, own_u), F32),
             spare((nu, wu, d), F32), spare((d, d), F32),
             spare((nu, own_i + TILE, d), jnp.int16), spare((nu, own_i + TILE, d), jnp.int16),
-            spare((d, own_i), F32),
+            spare((d, 2 * LANES), F32),
             spare((d, d), F32), spare((d, LANES), F32), spare((PANEL, d), F32),
             dma((nk,)), dma((4, ni)), dma((4, ni)), dma((1, nk)), dma((1, nk)),
             dma((3, slots + 1)), dma((3, slots + 1)), dma((3, nu)), dma((3, nu)),
@@ -575,7 +575,7 @@
     def lay(u_ref, i_ref, u_to, i_to):
         u_to[...] = u_ref[...]
         for k in range(0, nu, 2):
-            pair = jnp.concatenate([i_ref[k], i_ref[k + 1]], axis=1)
+            pair = jnp.concatenate([i_ref[k][:, :own_i], i_ref[k + 1][:, :own_i]], axis=1)
             i_to[:, k * own_i : (k + 2) * own_i] = pair
 
     u_new, i_new = pl.pallas_call(

time: 95.6 us -> 92.6 us (0.969)
  Pallas kernels: 94.1 us -> 91.1 us
    pallas_call x1, Pallas kernels: 92.3 us -> 89.3 us  [on_device(): pl.pallas_call(functools.partial(kernel, nu, ni), out_shape=(jax.ShapeDty...]
where the time goes in v3:
time: 92.6 us; the launch traced here: 92.4 us
  Pallas kernels  91.1 us (98%)
  between operations  1.29 us (1%)
    pallas_call x1, Pallas kernels, on_device(): pl.pallas_call(functools.partial(kernel, nu, ni), out_shape=(jax.ShapeDty...  89.3 us

profile of v3, /device:TPU:0, one launch (start us, length us, event | category | flops | bytes accessed | tf_op | source)
XLA Modules:
  0.0 92.4 jit_solution(7092459040440433)
XLA Ops:
  1.3 89.3 %shard_map.59 = (f32[16,2048]{1,0:T(8,128)}, f32[8,32,256]{2,1,0:T(8,128)}) custom-call(f32[1]{0:T(128)S(6)} %copy.6.alpha_ref, bf16[16,2048]{1,0:T(8,128)(2,1)} %bitcast.5, bf16[32,1536]{1,0:T(8,128)(2,1)} %bitcast.4, s32[2048,1536]{1,0:T(8,128)} %counts_hbm.1), custom_call_target="tpu_custom_call" | custom-call | tf_op jit(solution)/shard_map/pallas_call | solution.py:543
  90.6 1.8 %shard_map.60 = (f32[16,2048]{1,0:T(8,128)}, f32[32,1536]{1,0:T(8,128)}) custom-call(f32[16,2048]{1,0:T(8,128)} %get-tuple-element.6.u_ref, f32[8,32,256]{2,1,0:T(8,128)} %get-tuple-element.7.i_ref), custom_call_target="tpu_custom_call" | custom-call | tf_op jit(solution)/shard_map/pallas_call | solution.py:581

commit v4 on v3

--- a/solution.py
+++ b/solution.py
@@ -18,6 +18,7 @@
 LANES = 128
 TILE = 16
 STEPS_BESIDE = 6
+AHEAD = 4
 HOPS = (
     (1, 0, 0, 0, None, None),
     (-1, 0, 0, 0, None, None),
@@ -382,9 +383,18 @@
         rs1(off).start()
 
     sweep = Sweep(inv_a, inv_u, inv_y)
-    for work in user_pair(after(1)):
-        work()
-    halves(after(1)).start()
+    def plain_pass(off):
+        for work in user_pair(after(off)):
+            work()
+        halves(after(off)).start()
+
+    def plain_step(off, carry):
+        plain_pass(off)
+        on_to_owner(off - 1)
+        return carry
+
+    plain_pass(1)
+    lax.fori_loop(2, AHEAD + 1, plain_step, 0)
     each(ni, lambda off: gi_ag(off, from_item(off)).wait_recv())
 
     def hessian(gram):
@@ -393,13 +403,17 @@
     sweep.begin(hessian(gi))
 
     def first_pass(off, carry):
-        sweep.block(off - 2, user_pair(after(off)))
+        sweep.block(off - 1 - AHEAD, user_pair(after(off)))
         halves(after(off)).start()
         on_to_owner(off - 1)
         return carry
 
-    lax.fori_loop(2, nk + 1, first_pass, 0)
-    sweep.block(nk - 1)
+    def sweep_on(k, carry):
+        sweep.block(k)
+        return carry
+
+    lax.fori_loop(AHEAD + 1, nk + 1, first_pass, 0)
+    lax.fori_loop(nk - AHEAD, nk, sweep_on, 0)
     sweep.end(hessian(gi))
 
     halves(place).wait_recv()
@@ -485,10 +499,6 @@
     each(ni, lambda off: gu_ag(off, from_item(off)).wait_recv())
     each(nu, lambda off: rs2(nu - off).start())
     sweep.begin(hessian(gu))
-
-    def sweep_on(k, carry):
-        sweep.block(k)
-        return carry
 
     lax.fori_loop(0, d // PANEL, sweep_on, 0)
     sweep.end(hessian(gu))

time: 92.6 us -> 90.7 us (0.979)
  Pallas kernels: 91.1 us -> 89.3 us
    pallas_call x1, Pallas kernels: 89.3 us -> 87.5 us  [on_device(): pl.pallas_call(functools.partial(kernel, nu, ni), out_shape=(jax.ShapeDty...]
where the time goes in v4:
time: 90.7 us; the launch traced here: 90.6 us
  Pallas kernels  89.3 us (98%)
  between operations  1.29 us (1%)
    pallas_call x1, Pallas kernels, on_device(): pl.pallas_call(functools.partial(kernel, nu, ni), out_shape=(jax.ShapeDty...  87.5 us

profile of v4, /device:TPU:0, one launch (start us, length us, event | category | flops | bytes accessed | tf_op | source)
XLA Modules:
  0.0 90.6 jit_solution(1226577580430326508)
XLA Ops:
  1.3 87.5 %shard_map.59 = (f32[16,2048]{1,0:T(8,128)}, f32[8,32,256]{2,1,0:T(8,128)}) custom-call(f32[1]{0:T(128)S(6)} %copy.6.alpha_ref, bf16[16,2048]{1,0:T(8,128)(2,1)} %bitcast.5, bf16[32,1536]{1,0:T(8,128)(2,1)} %bitcast.4, s32[2048,1536]{1,0:T(8,128)} %counts_hbm.1), custom_call_target="tpu_custom_call" | custom-call | tf_op jit(solution)/shard_map/pallas_call | solution.py:553
  88.8 1.8 %shard_map.60 = (f32[16,2048]{1,0:T(8,128)}, f32[32,1536]{1,0:T(8,128)}) custom-call(f32[16,2048]{1,0:T(8,128)} %get-tuple-element.6.u_ref, f32[8,32,256]{2,1,0:T(8,128)} %get-tuple-element.7.i_ref), custom_call_target="tpu_custom_call" | custom-call | tf_op jit(solution)/shard_map/pallas_call | solution.py:591

commit v5 on v4

--- a/solution.py
+++ b/solution.py
@@ -18,7 +18,7 @@
 LANES = 128
 TILE = 16
 STEPS_BESIDE = 6
-AHEAD = 4
+AHEAD = 5
 HOPS = (
     (1, 0, 0, 0, None, None),
     (-1, 0, 0, 0, None, None),

time: 90.7 us -> 90.5 us (level)
  no operation moved by 1% of the time
where the time goes in v5:
time: 90.5 us; the launch traced here: 90.3 us
  Pallas kernels  89 us (98%)
  between operations  1.29 us (1%)
    pallas_call x1, Pallas kernels, on_device(): pl.pallas_call(functools.partial(kernel, nu, ni), out_shape=(jax.ShapeDty...  87.2 us

profile of v5, /device:TPU:0, one launch (start us, length us, event | category | flops | bytes accessed | tf_op | source)
XLA Modules:
  0.0 90.3 jit_solution(13111746769015320554)
XLA Ops:
  1.3 87.2 %shard_map.59 = (f32[16,2048]{1,0:T(8,128)}, f32[8,32,256]{2,1,0:T(8,128)}) custom-call(f32[1]{0:T(128)S(6)} %copy.6.alpha_ref, bf16[16,2048]{1,0:T(8,128)(2,1)} %bitcast.5, bf16[32,1536]{1,0:T(8,128)(2,1)} %bitcast.4, s32[2048,1536]{1,0:T(8,128)} %counts_hbm.1), custom_call_target="tpu_custom_call" | custom-call | tf_op jit(solution)/shard_map/pallas_call | solution.py:553
  88.5 1.8 %shard_map.60 = (f32[16,2048]{1,0:T(8,128)}, f32[32,1536]{1,0:T(8,128)}) custom-call(f32[16,2048]{1,0:T(8,128)} %get-tuple-element.6.u_ref, f32[8,32,256]{2,1,0:T(8,128)} %get-tuple-element.7.i_ref), custom_call_target="tpu_custom_call" | custom-call | tf_op jit(solution)/shard_map/pallas_call | solution.py:591
